TPU v7x, 32 devices: a whole 2x2x4 slice. The times are simulated.
32 devices in a mesh: groups: 2 (over x), dp: 8 (over z, y), tensor: 2 (over core).
Axes of the slice: x: 2, y: 2, z: 4, core: 2. Of those that a mesh axis runs over, the one named last changes fastest.
Arguments:
- queries: bfloat16 [2048, 8192], P(('groups', 'dp'), 'tensor'), parts along dimension 0
- response_key_rows: bfloat16 [2048, 1024], P(('groups', 'dp'), 'tensor'), parts along dimension 0
- response_value_rows: bfloat16 [2048, 1024], P(('groups', 'dp'), 'tensor'), parts along dimension 0, may hold values from -6 to 6
- shared_prompt_keys: bfloat16 [16, 768, 1024], P(('groups', 'dp'), None, 'tensor'), parts along dimension 0, may hold values from -6 to 6
- shared_prompt_values: bfloat16 [16, 768, 1024], P(('groups', 'dp'), None, 'tensor'), parts along dimension 0, may hold values from -6 to 6
- grad_out: bfloat16 [2048, 8192], P(('groups', 'dp'), 'tensor'), parts along dimension 0, may hold values from -6 to 6
- lengths: int32 [64], P('groups'), parts along dimension 0, may hold values from 1 to 64, as said below
- packing: int32 [16, 6], P(('groups', 'dp')), parts along dimension 0, may hold values from -1 to 31, as said below
- prompt_of: int32 [64], P('groups'), parts along dimension 0, may hold values from 0 to 7, as said below
- prompt_owner: int32 [16], P('groups'), parts along dimension 0, may hold values from 0 to 7, as said below
Outputs:
- attn_out: bfloat16 [2048, 8192], P(('groups', 'dp'), 'tensor'), parts along dimension 0
- grad_queries: bfloat16 [2048, 8192], P(('groups', 'dp'), 'tensor'), parts along dimension 0
- grad_response_keys: bfloat16 [2048, 1024], P(('groups', 'dp'), 'tensor'), parts along dimension 0
- grad_response_values: bfloat16 [2048, 1024], P(('groups', 'dp'), 'tensor'), parts along dimension 0
- grad_prompt_keys: bfloat16 [16, 768, 1024], P(('groups', 'dp'), None, 'tensor'), parts along dimension 0
- grad_prompt_values: bfloat16 [16, 768, 1024], P(('groups', 'dp'), None, 'tensor'), parts along dimension 0
There are 2 independent parts, one for each index of `groups`. A program takes and returns all parts, laid end to end along the dimension named above; each array names one. Nothing has to cross between parts.
Inputs may be any that keep to these rules, and one draw needn't show every extreme that they name: `prompt_of`: each prompt has exactly 4 responses. A permutation: prompt p sits at slot prompt_owner[p] of shared_prompt_keys and shared_prompt_values. `packing`: every response is named in exactly one list. List b names responses of the prompt at slot b first, then responses of the prompt at slot (b - 1) mod 8, then -1 entries; it names at least 2 responses. `lengths`: the responses of one list have 128 tokens or fewer together; some response has 64 tokens.
All inputs are finite; a program needn't handle non-finite values.
Results may differ from a plain program's by a relative error of at most 0.0035.
The roundings to bfloat16 on the way count: a program that leaves them out, or rounds other values in their place, can miss the bound.
Values may be sent and summed in bfloat16 or wider, within the bound.
No kernel may reach another device: no remote copies, remote signals or barrier semaphores. Data moves between devices by JAX's collectives and lax.ppermute only.
A program may use at most 64 MiB of HBM per device.

v0:
```python
from functools import partial

import jax
import jax.numpy as jnp
from jax import lax
from jax.sharding import PartitionSpec as P

HEAD_WIDTH = 128


NEGATIVE = -1e30


def from_behind(value, axis, steps):
    count = lax.axis_size(axis)
    pairs = [(source, (source + steps) % count) for source in range(count)]
    return lax.ppermute(value, axis, pairs)


def layout(entries, lengths, prompt_of, prompt_owner, device, devices, rows_here, prompt_len):
    lookup = jnp.arange(lengths.shape[0], dtype=jnp.int32)
    chosen = entries[:, None] == lookup[None, :]
    span_lengths = jnp.sum(jnp.where(chosen, lengths[None, :], 0), axis=1)
    prompts_here = jnp.sum(jnp.where(chosen, prompt_of[None, :], 0), axis=1)
    prompt_lookup = jnp.arange(prompt_owner.shape[0], dtype=jnp.int32)
    holders = jnp.sum(
        jnp.where(prompts_here[:, None] == prompt_lookup[None, :], prompt_owner[None, :], 0), axis=1
    )
    row_ends = jnp.cumsum(span_lengths)
    row_starts = row_ends - span_lengths
    row_index = jnp.arange(rows_here, dtype=jnp.int32)
    inside = (row_index[:, None] >= row_starts[None, :]) & (row_index[:, None] < row_ends[None, :])
    live_rows = jnp.any(inside, axis=1)
    slot_index = jnp.arange(entries.shape[0], dtype=jnp.int32)
    slot_of = jnp.where(live_rows, jnp.sum(jnp.where(inside, slot_index[None, :], 0), axis=1), -1)
    own_rows = jnp.any(inside & (holders == device)[None, :], axis=1)
    left_rows = jnp.any(inside & (holders == (device + devices - 1) % devices)[None, :], axis=1)
    causal = (
        (slot_of[:, None] == slot_of[None, :])
        & live_rows[:, None]
        & (row_index[None, :] <= row_index[:, None])
    )
    local_cols = causal | (row_index[:, None] == row_index[None, :])
    own_cols = jnp.broadcast_to(own_rows[:, None], (rows_here, prompt_len))
    left_cols = jnp.broadcast_to(left_rows[:, None], (rows_here, prompt_len))
    return (own_cols, left_cols, local_cols, live_rows)


def head_forward(allowed, operands):
    query_part, key_part, value_part = operands
    scores = jnp.einsum(
        "gtd,sd->gts", query_part, key_part, preferred_element_type=jnp.float32
    ) * HEAD_WIDTH ** (-0.5)
    scores = jnp.where(allowed[None], scores, NEGATIVE)
    row_max = jnp.max(scores, axis=-1, keepdims=True)
    exponent = jnp.exp(scores - row_max)
    row_sum = jnp.sum(exponent, axis=-1, keepdims=True)
    attention = exponent / row_sum
    weighted = jnp.einsum(
        "gts,sd->gtd",
        attention.astype(jnp.bfloat16),
        value_part,
        preferred_element_type=jnp.float32,
    )
    return (weighted, row_max, row_sum)


def head_backward(key_mask, operands):
    query_part, grad_part, dot_part, max_part, sum_part, key_part, value_part = operands
    score_scale = HEAD_WIDTH ** (-0.5)
    scores = (
        jnp.einsum("gtd,sd->gts", query_part, key_part, preferred_element_type=jnp.float32)
        * score_scale
    )
    scores = jnp.where(key_mask[None], scores, NEGATIVE)
    attention = jnp.exp(scores - max_part) / sum_part
    attention_low = attention.astype(jnp.bfloat16)
    grad_attention = jnp.einsum(
        "gtd,sd->gts", grad_part, value_part, preferred_element_type=jnp.float32
    )
    grad_low = (attention * (grad_attention - dot_part[..., None])).astype(jnp.bfloat16)
    grad_query = score_scale * jnp.einsum(
        "gts,sd->gtd", grad_low, key_part, preferred_element_type=jnp.float32
    )
    grad_key = score_scale * jnp.einsum(
        "gts,gtd->sd", grad_low, query_part, preferred_element_type=jnp.float32
    )
    grad_value = jnp.einsum(
        "gts,gtd->sd", attention_low, grad_part, preferred_element_type=jnp.float32
    )
    return (grad_query, grad_key, grad_value)


def per_device(
    queries,
    response_key_rows,
    response_value_rows,
    shared_prompt_keys,
    shared_prompt_values,
    grad_out,
    lengths,
    packing,
    prompt_of,
    prompt_owner,
):
    rows_here = queries.shape[0]
    kv_heads = response_key_rows.shape[1] // HEAD_WIDTH
    group_size = queries.shape[1] // (kv_heads * HEAD_WIDTH)
    prompt_len = shared_prompt_keys.shape[1]
    device = lax.axis_index("dp")
    devices = lax.axis_size("dp")
    own_cols, left_cols, local_cols, live_rows = layout(
        packing[0], lengths, prompt_of, prompt_owner, device, devices, rows_here, prompt_len
    )
    allowed = jnp.concatenate([own_cols, left_cols, local_cols], axis=1)
    own_keys = shared_prompt_keys[0]
    own_values = shared_prompt_values[0]
    left_keys, left_values = from_behind((own_keys, own_values), "dp", 1)

    def by_head(matrix):
        return jnp.transpose(matrix.reshape(matrix.shape[0], kv_heads, HEAD_WIDTH), (1, 0, 2))

    def rows_first(stacked):
        return jnp.transpose(stacked, (2, 0, 1, 3)).reshape(
            rows_here, kv_heads * group_size * HEAD_WIDTH
        )

    context_keys = by_head(jnp.concatenate([own_keys, left_keys, response_key_rows], axis=0))
    context_values = by_head(
        jnp.concatenate([own_values, left_values, response_value_rows], axis=0)
    )
    query_heads = jnp.transpose(
        queries.reshape(rows_here, kv_heads, group_size, HEAD_WIDTH), (1, 2, 0, 3)
    )
    weighted, row_max, row_sum = lax.map(
        partial(head_forward, allowed), (query_heads, context_keys, context_values)
    )
    live_mask = live_rows[:, None]
    result = jnp.where(live_mask, rows_first(weighted), 0.0).astype(jnp.bfloat16)
    grad_live = jnp.where(live_mask, grad_out, 0.0)
    row_dot = jnp.sum(
        grad_live.astype(jnp.float32).reshape(rows_here, kv_heads, group_size, HEAD_WIDTH)
        * result.astype(jnp.float32).reshape(rows_here, kv_heads, group_size, HEAD_WIDTH),
        axis=-1,
    )
    row_dot = jnp.transpose(row_dot, (1, 2, 0))
    grad_heads = jnp.transpose(
        grad_live.reshape(rows_here, kv_heads, group_size, HEAD_WIDTH), (1, 2, 0, 3)
    )
    grad_query, grad_key, grad_value = lax.map(
        partial(head_backward, allowed),
        (query_heads, grad_heads, row_dot, row_max, row_sum, context_keys, context_values),
    )
    back_key, back_value = from_behind(
        (grad_key[:, prompt_len : 2 * prompt_len], grad_value[:, prompt_len : 2 * prompt_len]),
        "dp",
        -1,
    )
    own_key = grad_key[:, :prompt_len]
    own_value = grad_value[:, :prompt_len]
    resident_key = grad_key[:, 2 * prompt_len :]
    resident_value = grad_value[:, 2 * prompt_len :]

    def key_rows(stacked):
        return (
            jnp.transpose(stacked, (1, 0, 2))
            .reshape(stacked.shape[1], kv_heads * HEAD_WIDTH)
            .astype(jnp.bfloat16)
        )

    prompt_key_gradient = key_rows(own_key + back_key)[None]
    prompt_value_gradient = key_rows(own_value + back_value)[None]
    return (
        result,
        rows_first(grad_query).astype(jnp.bfloat16),
        key_rows(resident_key),
        key_rows(resident_value),
        prompt_key_gradient,
        prompt_value_gradient,
    )


def solution(mesh):
    in_specs = (
        P(("groups", "dp"), "tensor"),
        P(("groups", "dp"), "tensor"),
        P(("groups", "dp"), "tensor"),
        P(("groups", "dp"), None, "tensor"),
        P(("groups", "dp"), None, "tensor"),
        P(("groups", "dp"), "tensor"),
        P("groups"),
        P(("groups", "dp"), None),
        P("groups"),
        P("groups"),
    )
    out_specs = (
        P(("groups", "dp"), "tensor"),
        P(("groups", "dp"), "tensor"),
        P(("groups", "dp"), "tensor"),
        P(("groups", "dp"), "tensor"),
        P(("groups", "dp"), None, "tensor"),
        P(("groups", "dp"), None, "tensor"),
    )
    return jax.shard_map(
        per_device, mesh=mesh, in_specs=in_specs, out_specs=out_specs, check_vma=False
    )
```

profile of v0, /device:TPU:0, one launch (start us, length us, event | category | flops | bytes accessed | tf_op | source)
XLA Modules:
  0.0 201.9 jit_solution(17269051332111460938)
XLA Ops:
  2.2 3.0 %collective-permute-start = (bf16[768,512]{0,1:T(8,128)(2,1)S(1)}, bf16[768,512]{0,1:T(8,128)(2,1)}, u32[]{:S(2)}, u32[]{:S(2)}) collective-permute-start(bf16[768,512]{0,1:T(8,128)(2,1)S(1)} %bitcast.179), channel_id=1, source_target_pairs={{0,2},{2,4},{4,6},{6,8},{8,10},{10,12},{12,14},{14,0},{1,3},{3,5},... | collective-permute-start | bytes 2359304 | tf_op jit(solution)/shard_map/ppermute | solution.py:17
  5.2 2.3 %copy.55 = bf16[1,768,512]{1,2,0:T(8,128)(2,1)} copy(bf16[1,768,512]{2,1,0:T(8,128)(2,1)} %param.18) | data formatting | bytes 1572864 | tf_op args[4]
  14.0 12.7 %collective-permute-done = bf16[768,512]{0,1:T(8,128)(2,1)} collective-permute-done((bf16[768,512]{0,1:T(8,128)(2,1)S(1)}, bf16[768,512]{0,1:T(8,128)(2,1)}, u32[]{:S(2)}, u32[]{:S(2)}) %collective-permute-start) | collective-permute-done | bytes 786464 | tf_op jit(solution)/shard_map/ppermute | solution.py:17
  28.2 2.3 %copy.59 = bf16[4,1664,128]{2,1,0:T(8,128)(2,1)} copy(bf16[4,1664,128]{1,2,0:T(8,128)(2,1)S(1)} %maximum_bitcast_fusion) | data formatting | bytes 3407872 | tf_op jit(solution)/shard_map/while | solution.py:135
  30.5 12.2 %collective-permute-done.1 = bf16[768,512]{0,1:T(8,128)(2,1)} collective-permute-done((bf16[768,512]{0,1:T(8,128)(2,1)}, bf16[768,512]{0,1:T(8,128)(2,1)}, u32[]{:S(2)}, u32[]{:S(2)}) %collective-permute-start.1) | collective-permute-done | bytes 786464 | tf_op jit(solution)/shard_map/ppermute | solution.py:17
  44.2 2.3 %copy.60 = bf16[4,1664,128]{2,1,0:T(8,128)(2,1)} copy(bf16[4,1664,128]{1,2,0:T(8,128)(2,1)S(1)} %maximum_bitcast_fusion.1) | data formatting | bytes 3407872 | tf_op jit(solution)/shard_map/while | solution.py:135
  46.8 30.3 %while.28 = (s32[]{:T(128)}, bf16[4,8,128,128]{3,2,1,0:T(8,128)(2,1)S(1)}, f32[4,8,128,1]{2,1,3,0:T(8,128)S(1)}, f32[4,8,128,1]{2,1,3,0:T(8,128)S(1)}, pred[128,...) while((s32[]{:T(128)}, ...), condition=%wide.region_11.12_spmd, body=%wide.region_8.11_spmd.sunk | while | flops 892860416 | bytes 22763616 | solution.py:135
  46.8 2.6 %fusion.77 = (f32[8,128]{1,0:T(8,128)S(1)}, f32[8,128,1664]{2,1,0:T(8,128)S(1)}) fusion(pred[128,1664]{1,0:T(8,128)(4,1)S(1)} %get-tuple-element.373, bf16[4,1664,128]{2,1,0:T(8,128)(2,1)} %get-tuple-element.375, s32[]{:T(128)} %get-tuple-element.360, bf16[4,8,128,128]{3,2,1,0:T(8,128)(2,1)S(1)} %get-tuple-element.374), kind=kOutput, calls=%fused_computation.3.clone.1 | convolution fusion | flops 441318400 | bytes 7721984 | tf_op jit(solution)/shard_map/while/body/eval_jaxpr/gtd,sd->gts/dot_general | solution.py:51
  51.1 3.3 %fusion.79 = bf16[4,8,128,128]{3,2,1,0:T(8,128)(2,1)S(1)} fusion(bf16[4,8,128,128]{3,2,1,0:T(8,128)(2,1)S(1)} %get-tuple-element.361, s32[]{:T(128)} %get-tuple-element.360, f32[8,128,1664]{2,1,0:T(8,128)S(1)} %get-tuple-element.333, f32[8,128]{1,0:T(8,128)S(1)} %fusion.78, f32[8,128]{1,0:T(8,128)S(1)} %get-tuple-element.334, ...), kind=kOutput, calls=%fused_computation.7.clone.1 | convolution fusion | flops 444727296 | bytes 7988224 | tf_op jit(solution)/shard_map/while/body/eval_jaxpr/gts,sd->gtd/dot_general | solution.py:59
  54.4 2.5 %fusion.77 = (f32[8,128]{1,0:T(8,128)S(1)}, f32[8,128,1664]{2,1,0:T(8,128)S(1)}) fusion(pred[128,1664]{1,0:T(8,128)(4,1)S(1)} %get-tuple-element.373, bf16[4,1664,128]{2,1,0:T(8,128)(2,1)} %get-tuple-element.375, s32[]{:T(128)} %get-tuple-element.360, bf16[4,8,128,128]{3,2,1,0:T(8,128)(2,1)S(1)} %get-tuple-element.374), kind=kOutput, calls=%fused_computation.3.clone.1 | convolution fusion | flops 441318400 | bytes 7721984 | tf_op jit(solution)/shard_map/while/body/eval_jaxpr/gtd,sd->gts/dot_general | solution.py:51
  58.7 3.3 %fusion.79 = bf16[4,8,128,128]{3,2,1,0:T(8,128)(2,1)S(1)} fusion(bf16[4,8,128,128]{3,2,1,0:T(8,128)(2,1)S(1)} %get-tuple-element.361, s32[]{:T(128)} %get-tuple-element.360, f32[8,128,1664]{2,1,0:T(8,128)S(1)} %get-tuple-element.333, f32[8,128]{1,0:T(8,128)S(1)} %fusion.78, f32[8,128]{1,0:T(8,128)S(1)} %get-tuple-element.334, ...), kind=kOutput, calls=%fused_computation.7.clone.1 | convolution fusion | flops 444727296 | bytes 7988224 | tf_op jit(solution)/shard_map/while/body/eval_jaxpr/gts,sd->gtd/dot_general | solution.py:59
  62.0 2.5 %fusion.77 = (f32[8,128]{1,0:T(8,128)S(1)}, f32[8,128,1664]{2,1,0:T(8,128)S(1)}) fusion(pred[128,1664]{1,0:T(8,128)(4,1)S(1)} %get-tuple-element.373, bf16[4,1664,128]{2,1,0:T(8,128)(2,1)} %get-tuple-element.375, s32[]{:T(128)} %get-tuple-element.360, bf16[4,8,128,128]{3,2,1,0:T(8,128)(2,1)S(1)} %get-tuple-element.374), kind=kOutput, calls=%fused_computation.3.clone.1 | convolution fusion | flops 441318400 | bytes 7721984 | tf_op jit(solution)/shard_map/while/body/eval_jaxpr/gtd,sd->gts/dot_general | solution.py:51
  66.2 3.3 %fusion.79 = bf16[4,8,128,128]{3,2,1,0:T(8,128)(2,1)S(1)} fusion(bf16[4,8,128,128]{3,2,1,0:T(8,128)(2,1)S(1)} %get-tuple-element.361, s32[]{:T(128)} %get-tuple-element.360, f32[8,128,1664]{2,1,0:T(8,128)S(1)} %get-tuple-element.333, f32[8,128]{1,0:T(8,128)S(1)} %fusion.78, f32[8,128]{1,0:T(8,128)S(1)} %get-tuple-element.334, ...), kind=kOutput, calls=%fused_computation.7.clone.1 | convolution fusion | flops 444727296 | bytes 7988224 | tf_op jit(solution)/shard_map/while/body/eval_jaxpr/gts,sd->gtd/dot_general | solution.py:59
  69.5 2.5 %fusion.77 = (f32[8,128]{1,0:T(8,128)S(1)}, f32[8,128,1664]{2,1,0:T(8,128)S(1)}) fusion(pred[128,1664]{1,0:T(8,128)(4,1)S(1)} %get-tuple-element.373, bf16[4,1664,128]{2,1,0:T(8,128)(2,1)} %get-tuple-element.375, s32[]{:T(128)} %get-tuple-element.360, bf16[4,8,128,128]{3,2,1,0:T(8,128)(2,1)S(1)} %get-tuple-element.374), kind=kOutput, calls=%fused_computation.3.clone.1 | convolution fusion | flops 441318400 | bytes 7721984 | tf_op jit(solution)/shard_map/while/body/eval_jaxpr/gtd,sd->gts/dot_general | solution.py:51
  73.8 3.3 %fusion.79 = bf16[4,8,128,128]{3,2,1,0:T(8,128)(2,1)S(1)} fusion(bf16[4,8,128,128]{3,2,1,0:T(8,128)(2,1)S(1)} %get-tuple-element.361, s32[]{:T(128)} %get-tuple-element.360, f32[8,128,1664]{2,1,0:T(8,128)S(1)} %get-tuple-element.333, f32[8,128]{1,0:T(8,128)S(1)} %fusion.78, f32[8,128]{1,0:T(8,128)S(1)} %get-tuple-element.334, ...), kind=kOutput, calls=%fused_computation.7.clone.1 | convolution fusion | flops 444727296 | bytes 7988224 | tf_op jit(solution)/shard_map/while/body/eval_jaxpr/gts,sd->gtd/dot_general | solution.py:59
  81.4 45.7 %while.29 = (s32[]{:T(128)}, bf16[4,8,128,128]{3,2,1,0:T(8,128)(2,1)S(1)}, f32[4,1664,128]{2,1,0:T(8,128)}, f32[4,1664,128]{2,1,0:T(8,128)}, pred[128,1664]{1,0:...) while((s32[]{:T(128)}, ...), condition=%wide.region_14.15_spmd, body=%wide.region_13.14_spmd.sunk | while | flops 2195013632 | bytes 35480708 | solution.py:150
  81.6 3.0 %exponential_divide_fusion.2 = f32[8,128,1664]{2,1,0:T(8,128)S(1)} fusion(f32[8,128]{1,0:T(8,128)S(1)} %get-tuple-element.349, f32[8,128]{1,0:T(8,128)S(1)} %get-tuple-element.350, pred[128,1664]{1,0:T(8,128)(4,1)S(1)} %get-tuple-element.408, bf16[4,1664,128]{2,1,0:T(8,128)(2,1)} %get-tuple-element.410, s32[]{:T(128)} %get-tuple-element.391, ...), kind=kOutput, calls=%fused_computation.22.clone.1 | convolution fusion | flops 443023360 | bytes 7726080 | tf_op jit(solution)/shard_map/while/body/eval_jaxpr/gtd,sd->gts/dot_general | solution.py:72
  84.6 2.2 %multiply_convert_fusion.2 = bf16[8,128,1664]{2,1,0:T(8,128)(2,1)S(1)} fusion(f32[8,128,1664]{2,1,0:T(8,128)S(1)} %exponential_divide_fusion.2, f32[8,128]{1,0:T(8,128)S(1)} %dynamic-slice_bitcast_fusion.6, bf16[4,1664,128]{2,1,0:T(8,128)(2,1)} %get-tuple-element.414, s32[]{:T(128)} %get-tuple-element.391, ...), kind=kOutput, calls=%fused_computation.21.clone.1 | convolution fusion | flops 441319424 | bytes 10916864 | tf_op jit(solution)/shard_map/while/body/eval_jaxpr/gtd,sd->gts/dot_general | solution.py:78
  88.9 2.1 %fusion.90 = bf16[4,8,128,128]{3,2,1,0:T(8,128)(2,1)S(1)} fusion(bf16[4,8,128,128]{3,2,1,0:T(8,128)(2,1)S(1)} %get-tuple-element.392, s32[]{:T(128)} %get-tuple-element.391, bf16[8,128,1664]{2,1,0:T(8,128)(2,1)S(1)} %multiply_convert_fusion.2, bf16[4,1664,128]{2,1,0:T(8,128)(2,1)} %get-tuple-element.410), kind=kOutput, calls=%fused_computation.33.clone.1 | convolution fusion | flops 436338688 | bytes 4359168 | tf_op jit(solution)/shard_map/while/body/eval_jaxpr/gts,sd->gtd/dot_general | solution.py:82
  93.0 3.0 %exponential_divide_fusion.2 = f32[8,128,1664]{2,1,0:T(8,128)S(1)} fusion(f32[8,128]{1,0:T(8,128)S(1)} %get-tuple-element.349, f32[8,128]{1,0:T(8,128)S(1)} %get-tuple-element.350, pred[128,1664]{1,0:T(8,128)(4,1)S(1)} %get-tuple-element.408, bf16[4,1664,128]{2,1,0:T(8,128)(2,1)} %get-tuple-element.410, s32[]{:T(128)} %get-tuple-element.391, ...), kind=kOutput, calls=%fused_computation.22.clone.1 | convolution fusion | flops 443023360 | bytes 7726080 | tf_op jit(solution)/shard_map/while/body/eval_jaxpr/gtd,sd->gts/dot_general | solution.py:72
  96.0 2.2 %multiply_convert_fusion.2 = bf16[8,128,1664]{2,1,0:T(8,128)(2,1)S(1)} fusion(f32[8,128,1664]{2,1,0:T(8,128)S(1)} %exponential_divide_fusion.2, f32[8,128]{1,0:T(8,128)S(1)} %dynamic-slice_bitcast_fusion.6, bf16[4,1664,128]{2,1,0:T(8,128)(2,1)} %get-tuple-element.414, s32[]{:T(128)} %get-tuple-element.391, ...), kind=kOutput, calls=%fused_computation.21.clone.1 | convolution fusion | flops 441319424 | bytes 10916864 | tf_op jit(solution)/shard_map/while/body/eval_jaxpr/gtd,sd->gts/dot_general | solution.py:78
  100.2 2.1 %fusion.90 = bf16[4,8,128,128]{3,2,1,0:T(8,128)(2,1)S(1)} fusion(bf16[4,8,128,128]{3,2,1,0:T(8,128)(2,1)S(1)} %get-tuple-element.392, s32[]{:T(128)} %get-tuple-element.391, bf16[8,128,1664]{2,1,0:T(8,128)(2,1)S(1)} %multiply_convert_fusion.2, bf16[4,1664,128]{2,1,0:T(8,128)(2,1)} %get-tuple-element.410), kind=kOutput, calls=%fused_computation.33.clone.1 | convolution fusion | flops 436338688 | bytes 4359168 | tf_op jit(solution)/shard_map/while/body/eval_jaxpr/gts,sd->gtd/dot_general | solution.py:82
  104.4 3.0 %exponential_divide_fusion.2 = f32[8,128,1664]{2,1,0:T(8,128)S(1)} fusion(f32[8,128]{1,0:T(8,128)S(1)} %get-tuple-element.349, f32[8,128]{1,0:T(8,128)S(1)} %get-tuple-element.350, pred[128,1664]{1,0:T(8,128)(4,1)S(1)} %get-tuple-element.408, bf16[4,1664,128]{2,1,0:T(8,128)(2,1)} %get-tuple-element.410, s32[]{:T(128)} %get-tuple-element.391, ...), kind=kOutput, calls=%fused_computation.22.clone.1 | convolution fusion | flops 443023360 | bytes 7726080 | tf_op jit(solution)/shard_map/while/body/eval_jaxpr/gtd,sd->gts/dot_general | solution.py:72
  107.4 2.2 %multiply_convert_fusion.2 = bf16[8,128,1664]{2,1,0:T(8,128)(2,1)S(1)} fusion(f32[8,128,1664]{2,1,0:T(8,128)S(1)} %exponential_divide_fusion.2, f32[8,128]{1,0:T(8,128)S(1)} %dynamic-slice_bitcast_fusion.6, bf16[4,1664,128]{2,1,0:T(8,128)(2,1)} %get-tuple-element.414, s32[]{:T(128)} %get-tuple-element.391, ...), kind=kOutput, calls=%fused_computation.21.clone.1 | convolution fusion | flops 441319424 | bytes 10916864 | tf_op jit(solution)/shard_map/while/body/eval_jaxpr/gtd,sd->gts/dot_general | solution.py:78
  111.6 2.1 %fusion.90 = bf16[4,8,128,128]{3,2,1,0:T(8,128)(2,1)S(1)} fusion(bf16[4,8,128,128]{3,2,1,0:T(8,128)(2,1)S(1)} %get-tuple-element.392, s32[]{:T(128)} %get-tuple-element.391, bf16[8,128,1664]{2,1,0:T(8,128)(2,1)S(1)} %multiply_convert_fusion.2, bf16[4,1664,128]{2,1,0:T(8,128)(2,1)} %get-tuple-element.410), kind=kOutput, calls=%fused_computation.33.clone.1 | convolution fusion | flops 436338688 | bytes 4359168 | tf_op jit(solution)/shard_map/while/body/eval_jaxpr/gts,sd->gtd/dot_general | solution.py:82
  115.7 3.0 %exponential_divide_fusion.2 = f32[8,128,1664]{2,1,0:T(8,128)S(1)} fusion(f32[8,128]{1,0:T(8,128)S(1)} %get-tuple-element.349, f32[8,128]{1,0:T(8,128)S(1)} %get-tuple-element.350, pred[128,1664]{1,0:T(8,128)(4,1)S(1)} %get-tuple-element.408, bf16[4,1664,128]{2,1,0:T(8,128)(2,1)} %get-tuple-element.410, s32[]{:T(128)} %get-tuple-element.391, ...), kind=kOutput, calls=%fused_computation.22.clone.1 | convolution fusion | flops 443023360 | bytes 7726080 | tf_op jit(solution)/shard_map/while/body/eval_jaxpr/gtd,sd->gts/dot_general | solution.py:72
  118.7 2.2 %multiply_convert_fusion.2 = bf16[8,128,1664]{2,1,0:T(8,128)(2,1)S(1)} fusion(f32[8,128,1664]{2,1,0:T(8,128)S(1)} %exponential_divide_fusion.2, f32[8,128]{1,0:T(8,128)S(1)} %dynamic-slice_bitcast_fusion.6, bf16[4,1664,128]{2,1,0:T(8,128)(2,1)} %get-tuple-element.414, s32[]{:T(128)} %get-tuple-element.391, ...), kind=kOutput, calls=%fused_computation.21.clone.1 | convolution fusion | flops 441319424 | bytes 10916864 | tf_op jit(solution)/shard_map/while/body/eval_jaxpr/gtd,sd->gts/dot_general | solution.py:78
  123.0 2.1 %fusion.90 = bf16[4,8,128,128]{3,2,1,0:T(8,128)(2,1)S(1)} fusion(bf16[4,8,128,128]{3,2,1,0:T(8,128)(2,1)S(1)} %get-tuple-element.392, s32[]{:T(128)} %get-tuple-element.391, bf16[8,128,1664]{2,1,0:T(8,128)(2,1)S(1)} %multiply_convert_fusion.2, bf16[4,1664,128]{2,1,0:T(8,128)(2,1)} %get-tuple-element.410), kind=kOutput, calls=%fused_computation.33.clone.1 | convolution fusion | flops 436338688 | bytes 4359168 | tf_op jit(solution)/shard_map/while/body/eval_jaxpr/gts,sd->gtd/dot_general | solution.py:82
  130.4 2.7 %slice.23 = f32[4,768,128]{2,1,0:T(8,128)} slice(f32[4,1664,128]{2,1,0:T(8,128)} %get-tuple-element.118), slice={[0:4], [768:1536], [0:128]} | slice | bytes 3145728 | tf_op jit(solution)/shard_map/slice | solution.py:155
  139.1 26.9 %collective-permute-done.3 = f32[4,768,128]{2,1,0:T(8,128)S(1)} collective-permute-done((f32[4,768,128]{2,1,0:T(8,128)S(1)}, f32[4,768,128]{2,1,0:T(8,128)S(1)}, u32[]{:S(2)}, u32[]{:S(2)}) %collective-permute-start.3) | collective-permute-done | bytes 1572896 | tf_op jit(solution)/shard_map/ppermute | solution.py:17
  169.4 28.7 %collective-permute-done.2 = f32[4,768,128]{2,1,0:T(8,128)} collective-permute-done((f32[4,768,128]{2,1,0:T(8,128)}, f32[4,768,128]{2,1,0:T(8,128)}, u32[]{:S(2)}, u32[]{:S(2)}) %collective-permute-start.2) | collective-permute-done | bytes 1572896 | tf_op jit(solution)/shard_map/ppermute | solution.py:17
  198.1 2.0 %fusion.49 = bf16[768,4,128]{2,0,1:T(8,128)(2,1)S(1)} fusion(f32[4,768,128]{2,1,0:T(8,128)} %collective-permute-done.2, f32[4,1664,128]{2,1,0:T(8,128)} %get-tuple-element.118), kind=kLoop, calls=%fused_computation.69 | loop fusion | flops 786432 | bytes 3932160 | tf_op jit(solution)/shard_map/convert_element_type | solution.py:168
  (76 shorter events, 53.1 us)
Async XLA Ops:
  0.6 11.6 %copy-start.3 = (bf16[128,512]{1,0:T(8,128)(2,1)S(1)}, bf16[128,512]{1,0:T(8,128)(2,1)}, u32[]{:S(2)}) copy-start(bf16[128,512]{1,0:T(8,128)(2,1)} %param.16) | copy-start | bytes 393220
  0.6 11.7 %copy-start.2 = (bf16[128,4096]{1,0:T(8,128)(2,1)S(1)}, bf16[128,4096]{1,0:T(8,128)(2,1)}, u32[]{:S(2)}) copy-start(bf16[128,4096]{1,0:T(8,128)(2,1)} %param.14) | copy-start | bytes 3145732
  2.2 11.9 %copy-start = (bf16[1,768,512]{1,2,0:T(8,128)(2,1)}, bf16[1,768,512]{1,2,0:T(8,128)(2,1)S(1)}, u32[]{:S(2)}) copy-start(bf16[1,768,512]{1,2,0:T(8,128)(2,1)S(1)} %copy.52) | copy-start | bytes 2359300
  2.2 24.5 %collective-permute-start = (bf16[768,512]{0,1:T(8,128)(2,1)S(1)}, bf16[768,512]{0,1:T(8,128)(2,1)}, u32[]{:S(2)}, u32[]{:S(2)}) collective-permute-start(bf16[768,512]{0,1:T(8,128)(2,1)S(1)} %bitcast.179), channel_id=1, source_target_pairs={{0,2},{2,4},{4,6},{6,8},{8,10},{10,12},{12,14},{14,0},{1,3},{3,5},... | collective-permute-start | bytes 2359304 | tf_op jit(solution)/shard_map/ppermute | solution.py:17
  7.5 35.3 %collective-permute-start.1 = (bf16[768,512]{0,1:T(8,128)(2,1)}, bf16[768,512]{0,1:T(8,128)(2,1)}, u32[]{:S(2)}, u32[]{:S(2)}) collective-permute-start(bf16[768,512]{0,1:T(8,128)(2,1)} %bitcast.33), channel_id=1, source_target_pairs={{0,2},{2,4},{4,6},{6,8},{8,10},{10,12},{12,14},{14,0},{1,3},{3,5},... | collective-permute-start | bytes 2359304 | tf_op jit(solution)/shard_map/ppermute | solution.py:17
  46.7 31.0 %copy-start.1 = (bf16[128,4096]{1,0:T(8,128)(2,1)S(1)}, bf16[128,4096]{1,0:T(8,128)(2,1)}, u32[]{:S(2)}) copy-start(bf16[128,4096]{1,0:T(8,128)(2,1)} %param.19) | copy-start | bytes 3145732
  128.6 37.4 %collective-permute-start.3 = (f32[4,768,128]{2,1,0:T(8,128)S(1)}, f32[4,768,128]{2,1,0:T(8,128)S(1)}, u32[]{:S(2)}, u32[]{:S(2)}) collective-permute-start(f32[4,768,128]{2,1,0:T(8,128)S(1)} %slice.25), channel_id=1, source_target_pairs={{0,14},{2,0},{4,2},{6,4},{8,6},{10,8},{12,10},{14,12},{1,15},{3,1}... | collective-permute-start | bytes 4718600 | tf_op jit(solution)/shard_map/ppermute | solution.py:17
  133.2 64.9 %collective-permute-start.2 = (f32[4,768,128]{2,1,0:T(8,128)}, f32[4,768,128]{2,1,0:T(8,128)}, u32[]{:S(2)}, u32[]{:S(2)}) collective-permute-start(f32[4,768,128]{2,1,0:T(8,128)} %slice.23), channel_id=1, source_target_pairs={{0,14},{2,0},{4,2},{6,4},{8,6},{10,8},{12,10},{14,12},{1,15},{3,1}... | collective-permute-start | bytes 4718600 | tf_op jit(solution)/shard_map/ppermute | solution.py:17
where the time goes:
time: 203 us; the launch traced here: 202 us
  waiting for transfers between devices  80.5 us (40%)
  matrix products  68.6 us (34%)
  local copies, waits for them, and re-layouts  25.3 us (12%)
  other arithmetic  18.6 us (9%)
  starting transfers between devices  7.74 us (4%)
    ppermute x4, waiting for transfers between devices, from_behind(): return lax.ppermute(value, axis, pairs)  80.5 us
    dot_general x4, matrix products, head_forward(): jnp.einsum('gts,sd->gtd', attention.astype(jnp.bfloat16), value_part, pre...  13.1 us
    dot_general x4, matrix products, head_backward(): jnp.einsum('gtd,sd->gts', query_part, key_part, preferred_element_type=jn...  11.9 us
    dot_general x4, matrix products, head_forward(): jnp.einsum('gtd,sd->gts', query_part, key_part, preferred_element_type=jn...  10.2 us
    dot_general x4, matrix products, head_backward(): jnp.einsum('gtd,sd->gts', grad_part, value_part, preferred_element_type=j...  8.82 us
    dot_general x4, matrix products, head_backward(): jnp.einsum('gts,sd->gtd', grad_low, key_part, preferred_element_type=jnp....  8.46 us
    unnamed x16, local copies, waits for them, and re-layouts  8.33 us
    dot_general x4, matrix products, head_backward(): jnp.einsum('gts,gtd->sd', attention_low, grad_part, preferred_element_typ...  8.13 us
  transfers between devices with their start and end apart: 4, of which 4 were waited for; matrix products, arithmetic and copies ran while one was open for 11% of the time, Pallas kernels for 0%

commit v1 on v0

v1 whole, which is shorter than its diff:
```python
import functools

import jax
import jax.numpy as jnp
from jax import lax
from jax.experimental import pallas as pl
from jax.experimental.pallas import tpu as pltpu
from jax.sharding import PartitionSpec as P

HEAD_WIDTH = 128
TILE_ROWS = 32
SCORE_SCALE = HEAD_WIDTH ** -0.5
LOG2_E = 1.4426950408889634
NEGATIVE = -1e30
F32 = jnp.float32
BF16 = jnp.bfloat16
VMEM_LIMIT = 48 * 1024 * 1024


def shifted(value, axis, steps):
    count = lax.axis_size(axis)
    pairs = [(source, (source + steps) % count) for source in range(count)]
    return lax.ppermute(value, axis, pairs)


def dot(left, right):
    return lax.dot_general(
        left, right, (((1,), (0,)), ((), ())), preferred_element_type=F32
    )


def plan(scalars):
    device, packing, lengths, prompt_of, prompt_owner = scalars
    own = jnp.int32(0)
    total = jnp.int32(0)
    ends = []
    for slot in range(packing.shape[1]):
        entry = packing[0, slot]
        used = entry >= 0
        index = jnp.maximum(entry, 0)
        length = jnp.where(used, lengths[index], 0)
        holder = prompt_owner[prompt_of[index]]
        own = own + jnp.where(holder == device[0], length, 0)
        total = total + length
        ends.append(total)
    return own, total, ends


def tile_of(ref, row, group):
    rows = ref[pl.ds(row, TILE_ROWS), :]
    return jnp.concatenate(
        [rows[:, g * HEAD_WIDTH : (g + 1) * HEAD_WIDTH] for g in range(group)], axis=0
    )


def put_tile(ref, row, group, value):
    for g in range(group):
        ref[pl.ds(row, TILE_ROWS), g * HEAD_WIDTH : (g + 1) * HEAD_WIDTH] = value[
            g * TILE_ROWS : (g + 1) * TILE_ROWS
        ]


def local_mask(first_row, ends, keys, columns):
    column = lax.broadcasted_iota(jnp.int32, (1, columns), 1)
    row = first_row + lax.rem(column, TILE_ROWS)
    start = jnp.zeros((1, columns), jnp.int32)
    for end in ends:
        start = jnp.where(row >= end, end, start)
    key = lax.broadcasted_iota(jnp.int32, (keys, columns), 0)
    return (key >= start) & (key <= row)


def gather_kernel(*refs):
    scalars, (query, grad, rows_out, count_out) = refs[:5], refs[5:]
    own, total, _ = plan(scalars)
    rows = query.shape[0]
    target = lax.broadcasted_iota(jnp.int32, (rows, rows), 0)
    source = lax.broadcasted_iota(jnp.int32, (rows, rows), 1)
    pick = ((source == target + own) & (source < total)).astype(BF16)
    rows_out[0] = dot(pick, query[...]).astype(BF16)
    rows_out[1] = dot(pick, grad[...]).astype(BF16)
    count_out[...] = jnp.full(count_out.shape, total - own, jnp.int32)


def segment(
    count, offset, ends, query_tile, grad_tile, keys, values, local_keys, local_values,
    group, put, key_acc, value_acc, local_key_acc, local_value_acc,
):
    columns = group * TILE_ROWS
    keys_t = keys.T
    values_t = values.T
    local_keys_t = local_keys.T
    local_values_t = local_values.T
    scale2 = SCORE_SCALE * LOG2_E

    def body(tile, carry):
        row = pl.multiple_of(tile * TILE_ROWS, TILE_ROWS)
        within = row + lax.rem(lax.broadcasted_iota(jnp.int32, (columns, 1), 0), TILE_ROWS)
        query = jnp.where(within < count, query_tile(row), 0)
        grad = jnp.where(within < count, grad_tile(row), 0)
        query_t = query.T
        grad_t = grad.T
        within_t = row + lax.rem(lax.broadcasted_iota(jnp.int32, (1, columns), 1), TILE_ROWS)
        allowed = local_mask(row + offset, ends, local_keys.shape[0], columns)
        scores = dot(keys, query_t) * scale2
        local_scores = jnp.where(allowed, dot(local_keys, query_t) * scale2, NEGATIVE)
        top = jnp.maximum(
            jnp.max(scores, axis=0, keepdims=True), jnp.max(local_scores, axis=0, keepdims=True)
        )
        weight = jnp.exp2(scores - top)
        local_weight = jnp.exp2(local_scores - top)
        inverse = 1.0 / (
            jnp.sum(weight, axis=0, keepdims=True) + jnp.sum(local_weight, axis=0, keepdims=True)
        )
        weight = weight * inverse
        local_weight = local_weight * inverse
        weight_low = weight.astype(BF16)
        local_weight_low = local_weight.astype(BF16)
        out_t = dot(values_t, weight_low) + dot(local_values_t, local_weight_low)
        out_t = jnp.where(within_t < count, out_t, 0.0).astype(BF16)
        row_dot = jnp.sum(out_t.astype(F32) * grad_t.astype(F32), axis=0, keepdims=True)
        grad_scores = (weight * (dot(values, grad_t) - row_dot)).astype(BF16)
        local_grad_scores = (local_weight * (dot(local_values, grad_t) - row_dot)).astype(BF16)
        grad_query_t = (
            dot(keys_t, grad_scores) + dot(local_keys_t, local_grad_scores)
        ) * SCORE_SCALE
        if key_acc is not None:
            key_acc[...] += dot(grad_scores, query) * SCORE_SCALE
            value_acc[...] += dot(weight_low, grad)
        local_key_acc[...] += dot(local_grad_scores, query) * SCORE_SCALE
        local_value_acc[...] += dot(local_weight_low, grad)
        put(tile, row, out_t.T, grad_query_t.astype(BF16).T, top, inverse, row_dot)
        return carry

    lax.fori_loop(0, lax.div(count + TILE_ROWS - 1, TILE_ROWS), body, 0)


def own_kernel(*refs):
    scalars = refs[:5]
    (query, grad, keys, values, local_keys, local_values, out, grad_query, local_key, local_value,
     key_part, value_part) = refs[5:]
    own, _, ends = plan(scalars)
    group = query.shape[1] // HEAD_WIDTH
    for ref in (out, grad_query, local_key, local_value, key_part, value_part):
        ref[...] = jnp.zeros(ref.shape, ref.dtype)

    def put(tile, row, out_tile, grad_query_tile, top, inverse, row_dot):
        put_tile(out, row, group, out_tile)
        put_tile(grad_query, row, group, grad_query_tile)

    segment(
        own, 0, ends,
        lambda row: tile_of(query, row, group), lambda row: tile_of(grad, row, group),
        keys[...], values[...], local_keys[...], local_values[...],
        group, put, key_part, value_part, local_key, local_value,
    )


def left_kernel(*refs):
    scalars = refs[:5]
    (rows, keys, values, local_keys, local_values, own_out, own_grad_query, own_local_key,
     own_local_value, out, grad_query, local_key, local_value, stats,
     left_out, left_grad_query, key_acc, value_acc) = refs[5:]
    own, total, ends = plan(scalars)
    head = pl.program_id(0)
    group = rows.shape[2] // HEAD_WIDTH
    columns = group * TILE_ROWS
    count = rows.shape[1]
    left_out[...] = jnp.zeros(left_out.shape, BF16)
    left_grad_query[...] = jnp.zeros(left_grad_query.shape, BF16)
    key_acc[...] = own_local_key[...]
    value_acc[...] = own_local_value[...]

    @pl.when(head == 0)
    def _():
        stats[...] = jnp.zeros(stats.shape, F32)

    def put(tile, row, out_tile, grad_query_tile, top, inverse, row_dot):
        put_tile(left_out, row, group, out_tile)
        put_tile(left_grad_query, row, group, grad_query_tile)
        for index, value in enumerate((top, inverse, row_dot)):
            stats[pl.ds(head * 4 + index, 1), pl.ds(pl.multiple_of(tile * columns, columns), columns)] = value

    segment(
        total - own, own, ends,
        lambda row: tile_of(rows.at[0], row, group), lambda row: tile_of(rows.at[1], row, group),
        keys[...], values[...], local_keys[...], local_values[...],
        group, put, None, None, key_acc, value_acc,
    )
    target = lax.broadcasted_iota(jnp.int32, (count, count), 0)
    source = lax.broadcasted_iota(jnp.int32, (count, count), 1)
    place = (target == source + own).astype(BF16)
    out[...] = (own_out[...].astype(F32) + dot(place, left_out[...])).astype(BF16)
    grad_query[...] = (own_grad_query[...].astype(F32) + dot(place, left_grad_query[...])).astype(BF16)
    local_key[...] = key_acc[...].astype(BF16)
    local_value[...] = value_acc[...].astype(BF16)


def arrived_kernel(count, rows, stats, keys, values, own_key, own_value, key_out, value_out,
                   key_acc, value_acc):
    head = pl.program_id(0)
    group = rows.shape[2] // HEAD_WIDTH
    columns = group * TILE_ROWS
    scale2 = SCORE_SCALE * LOG2_E
    key_acc[...] = own_key[...]
    value_acc[...] = own_value[...]

    def body(tile, carry):
        row = pl.multiple_of(tile * TILE_ROWS, TILE_ROWS)
        query = tile_of(rows.at[0], row, group)
        grad = tile_of(rows.at[1], row, group)
        where = pl.ds(pl.multiple_of(tile * columns, columns), columns)
        top = stats[pl.ds(head * 4, 1), where]
        inverse = stats[pl.ds(head * 4 + 1, 1), where]
        row_dot = stats[pl.ds(head * 4 + 2, 1), where]
        weight = jnp.exp2(dot(keys[...], query.T) * scale2 - top) * inverse
        grad_scores = (weight * (dot(values[...], grad.T) - row_dot)).astype(BF16)
        key_acc[...] += dot(grad_scores, query) * SCORE_SCALE
        value_acc[...] += dot(weight.astype(BF16), grad)
        return carry

    lax.fori_loop(0, lax.div(count[0, 0] + TILE_ROWS - 1, TILE_ROWS), body, 0)
    key_out[0] = key_acc[...].astype(BF16)
    value_out[0] = value_acc[...].astype(BF16)


def per_device(
    queries, response_key_rows, response_value_rows, shared_prompt_keys, shared_prompt_values,
    grad_out, lengths, packing, prompt_of, prompt_owner,
):
    rows = queries.shape[0]
    kv_heads = response_key_rows.shape[1] // HEAD_WIDTH
    width = queries.shape[1] // kv_heads
    prompt = shared_prompt_keys.shape[1]
    device = lax.axis_index("dp").astype(jnp.int32).reshape(1)
    scalars = (device, packing, lengths, prompt_of, prompt_owner)
    smem = [pl.BlockSpec(memory_space=pltpu.SMEM)] * 5
    params = pltpu.CompilerParams(vmem_limit_bytes=VMEM_LIMIT)
    shape = jax.ShapeDtypeStruct
    wide = pl.BlockSpec((rows, width), lambda h: (0, h))
    narrow = pl.BlockSpec((rows, HEAD_WIDTH), lambda h: (0, h))
    context = pl.BlockSpec((prompt, HEAD_WIDTH), lambda h: (0, h))
    pair = pl.BlockSpec((2, rows, width), lambda h: (0, 0, h))
    own_keys = shared_prompt_keys[0]
    own_values = shared_prompt_values[0]
    stat_columns = rows * width // HEAD_WIDTH
    stat_block = pl.BlockSpec((4 * kv_heads, stat_columns), lambda h: (0, 0))

    left_keys = shifted(own_keys, "dp", 1)
    left_values = shifted(own_values, "dp", 1)

    moved, count = pl.pallas_call(
        gather_kernel,
        grid=(kv_heads,),
        in_specs=smem + [wide, wide],
        out_specs=[pair, pl.BlockSpec((8, 128), lambda h: (0, 0))],
        out_shape=[shape((2, rows, queries.shape[1]), BF16), shape((8, 128), jnp.int32)],
        compiler_params=params,
        name="gather_rows",
    )(*scalars, queries, grad_out)
    arrived_count = shifted(count, "dp", -1)
    arrived = shifted(moved, "dp", -1)

    own_out, own_grad_query, own_local_key, own_local_value, own_key, own_value = pl.pallas_call(
        own_kernel,
        grid=(kv_heads,),
        in_specs=smem + [wide, wide, context, context, narrow, narrow],
        out_specs=[wide, wide, narrow, narrow, context, context],
        out_shape=[
            shape(queries.shape, BF16), shape(queries.shape, BF16),
            shape(response_key_rows.shape, F32), shape(response_key_rows.shape, F32),
            shape(own_keys.shape, F32), shape(own_keys.shape, F32),
        ],
        compiler_params=params,
        name="own_rows",
    )(*scalars, queries, grad_out, own_keys, own_values, response_key_rows, response_value_rows)

    out, grad_query, local_key, local_value, stats = pl.pallas_call(
        left_kernel,
        grid=(kv_heads,),
        in_specs=smem + [pair, context, context, narrow, narrow, wide, wide, narrow, narrow],
        out_specs=[wide, wide, narrow, narrow, stat_block],
        out_shape=[
            shape(queries.shape, BF16), shape(queries.shape, BF16),
            shape(response_key_rows.shape, BF16), shape(response_key_rows.shape, BF16),
            shape((4 * kv_heads, stat_columns), F32),
        ],
        scratch_shapes=[
            pltpu.VMEM((rows, width), BF16), pltpu.VMEM((rows, width), BF16),
            pltpu.VMEM((rows, HEAD_WIDTH), F32), pltpu.VMEM((rows, HEAD_WIDTH), F32),
        ],
        compiler_params=params,
        name="left_rows",
    )(*scalars, moved, left_keys, left_values, response_key_rows, response_value_rows,
      own_out, own_grad_query, own_local_key, own_local_value)
    arrived_stats = shifted(stats, "dp", -1)

    whole = pl.BlockSpec((1, prompt, HEAD_WIDTH), lambda h: (0, 0, h))
    prompt_key, prompt_value = pl.pallas_call(
        arrived_kernel,
        grid=(kv_heads,),
        in_specs=[pl.BlockSpec(memory_space=pltpu.SMEM), pair, stat_block, context, context, context, context],
        out_specs=[whole, whole],
        out_shape=[shape((1,) + own_keys.shape, BF16)] * 2,
        scratch_shapes=[pltpu.VMEM((prompt, HEAD_WIDTH), F32)] * 2,
        compiler_params=params,
        name="arrived_rows",
    )(arrived_count, arrived, arrived_stats, own_keys, own_values, own_key, own_value)
    return out, grad_query, local_key, local_value, prompt_key, prompt_value


def solution(mesh):
    rows = P(("groups", "dp"), "tensor")
    prompts = P(("groups", "dp"), None, "tensor")
    in_specs = (
        rows, rows, rows, prompts, prompts, rows,
        P("groups"), P(("groups", "dp"), None), P("groups"), P("groups"),
    )
    out_specs = (rows, rows, rows, rows, prompts, prompts)
    return jax.shard_map(
        per_device, mesh=mesh, in_specs=in_specs, out_specs=out_specs, check_vma=False
    )
```

time: 203 us -> 124 us (0.61)
  the two profiles are of different devices: /device:TPU:0 before, /device:TPU:16 now
where the time goes in v1:
time: 124 us
  waiting for transfers between devices  68.1 us (55%)
  Pallas kernels  41.5 us (33%)
  starting transfers between devices  6.96 us (6%)
  local copies, waits for them, and re-layouts  6.41 us (5%)
    ppermute x5, waiting for transfers between devices, shifted(): return lax.ppermute(value, axis, pairs)  68.1 us
    pallas_call x1, Pallas kernels, per_device(): pl.pallas_call(own_kernel, grid=(kv_heads,), in_specs=smem + [wide, wide,...  15.2 us
    pallas_call x1, Pallas kernels, per_device(): pl.pallas_call(left_kernel, grid=(kv_heads,), in_specs=smem + [pair, cont...  14.5 us
    pallas_call x1, Pallas kernels, per_device(): pl.pallas_call(arrived_kernel, grid=(kv_heads,), in_specs=[pl.BlockSpec(m...  9.64 us
    ppermute x5, starting transfers between devices, shifted(): return lax.ppermute(value, axis, pairs)  6.96 us
    unnamed x28, local copies, waits for them, and re-layouts  6.41 us
  transfers between devices with their start and end apart: 5, of which 3 were waited for; matrix products, arithmetic and copies ran while one was open for 0% of the time, Pallas kernels for 24%

profile of v1, /device:TPU:16, one launch (start us, length us, event | category | flops | bytes accessed | tf_op | source)
XLA Modules:
  0.0 123.6 jit_solution(2928790039398311248)
XLA Ops:
  0.6 0.0 copy-start
  0.6 1.2 copy-done
  1.9 0.0 copy-start.1
  1.9 1.2 copy-done.1
  3.1 0.0 copy-start.9
  3.1 0.7 copy-done.9
  3.7 0.7 copy-done.10
  4.4 0.7 copy-done.11
  5.1 0.7 copy-done.12
  5.7 2.1 %gather_rows.1 = (bf16[2,128,4096]{2,1,0:T(8,128)(2,1)S(1)}, s32[8,128]{1,0:T(8,128)S(1)}) custom-call(s32[1]{0:T(128)} %bitcast.refs_0_, s32[1,6]{1,0:T(1,128)S(1)} %copy-done.9, s32[32]{0:T(128)S(1)} %copy-done.10, s32[32]{0:T(128)S(1)} %copy-done.11, s32[8]{0:T(128)S(1)} %copy-done.12, bf16[128,4096]{1,0:T(8,128)(2,1)S(1)} %copy-done, ...), custom_call_target="tpu_custom_call" | custom-call | tf_op jit(solution)/shard_map/gather_rows/pallas_call | solution.py:252
  7.8 0.0 copy-start.4
  7.8 1.5 %collective-permute-start.3 = (bf16[2,128,4096]{2,1,0:T(8,128)(2,1)S(1)}, bf16[2,128,4096]{2,1,0:T(8,128)(2,1)S(1)}, u32[]{:S(2)}, u32[]{:S(2)}) collective-permute-start(bf16[2,128,4096]{2,1,0:T(8,128)(2,1)S(1)} %get-tuple-element.21.refs_5_), channel_id=1, source_target_pairs={{0,14},{2,0},{4,2},{6,4},{8,6},{10,8},{12,10},{14,12},{1,15},{3,1}... | collective-permute-start | bytes 6291464 | tf_op jit(solution)/shard_map/ppermute | solution.py:23
  9.3 0.0 copy-done.2
  9.3 0.6 collective-permute-start
  9.9 0.0 copy-done.3
  9.9 2.4 %collective-permute-start.1 = (bf16[768,512]{1,0:T(8,128)(2,1)S(1)}, bf16[768,512]{1,0:T(8,128)(2,1)S(1)}, u32[]{:S(2)}, u32[]{:S(2)}) collective-permute-start(bf16[768,512]{1,0:T(8,128)(2,1)S(1)} %bitcast.6), channel_id=1, source_target_pairs={{0,2},{2,4},{4,6},{6,8},{8,10},{10,12},{12,14},{14,0},{1,3},{3,5},... | collective-permute-start | bytes 2359304 | tf_op jit(solution)/shard_map/ppermute | solution.py:23
  12.3 0.0 copy-done.7
  12.3 0.0 copy-done.8
  12.3 15.2 %own_rows.1 = (bf16[128,4096]{1,0:T(8,128)(2,1)S(1)}, bf16[128,4096]{1,0:T(8,128)(2,1)S(1)}, f32[128,512]{1,0:T(8,128)S(1)}, f32[128,512]{1,0:T(8,128)S(1)}, f32[768,512]{1,0:T(8,128)}, /*index=5*/f32[768,512]{1,0:T(8,128)}) custom-call(s32[1]{0:T(128)} %bitcast.refs_0_, s32[1,6]{1,0:T(1,128)S(1)} %copy-done.9, s32[32]{0:T(128)S(1)} %copy-done.10, ...), custom_call_target="tpu_custom_call" | custom-call | tf_op jit(solution)/shard_map/own_rows/pallas_call | solution.py:264
  27.6 44.6 %collective-permute-done.refs_6_ = bf16[768,512]{1,0:T(8,128)(2,1)S(1)} collective-permute-done((bf16[768,512]{1,0:T(8,128)(2,1)S(1)}, bf16[768,512]{1,0:T(8,128)(2,1)S(1)}, u32[]{:S(2)}, u32[]{:S(2)}) %collective-permute-start) | collective-permute-done | bytes 786464 | tf_op jit(solution)/shard_map/ppermute | solution.py:23
  72.2 16.0 %collective-permute-done.1.refs_7_ = bf16[768,512]{1,0:T(8,128)(2,1)S(1)} collective-permute-done((bf16[768,512]{1,0:T(8,128)(2,1)S(1)}, bf16[768,512]{1,0:T(8,128)(2,1)S(1)}, u32[]{:S(2)}, u32[]{:S(2)}) %collective-permute-start.1) | collective-permute-done | bytes 786464 | tf_op jit(solution)/shard_map/ppermute | solution.py:23
  88.2 0.0 copy-done.4
  88.2 14.5 %left_rows.1 = (bf16[128,4096]{1,0:T(8,128)(2,1)}, bf16[128,4096]{1,0:T(8,128)(2,1)}, bf16[128,512]{1,0:T(8,128)(2,1)}, bf16[128,512]{1,0:T(8,128)(2,1)}, f32[16,1024]{1,0:T(8,128)S(1)}) custom-call(s32[1]{0:T(128)} %bitcast.refs_0_, s32[1,6]{1,0:T(1,128)S(1)} %copy-done.9, s32[32]{0:T(128)S(1)} %copy-done.10, s32[32]{0:T(128)S(1)} %copy-done.11, ...), custom_call_target="tpu_custom_call" | custom-call | tf_op jit(solution)/shard_map/left_rows/pallas_call | solution.py:278
  102.8 2.4 %collective-permute-start.4 = (f32[16,1024]{1,0:T(8,128)S(1)}, f32[16,1024]{1,0:T(8,128)S(1)}, u32[]{:S(2)}, u32[]{:S(2)}) collective-permute-start(f32[16,1024]{1,0:T(8,128)S(1)} %get-tuple-element.31), channel_id=1, source_target_pairs={{0,14},{2,0},{4,2},{6,4},{8,6},{10,8},{12,10},{14,12},{1,15},{3,1}... | collective-permute-start | bytes 196616 | tf_op jit(solution)/shard_map/ppermute | solution.py:23
  105.2 0.1 collective-permute-start.2
  105.2 7.4 %collective-permute-done.2.count = s32[8,128]{1,0:T(8,128)S(1)} collective-permute-done((s32[8,128]{1,0:T(8,128)S(1)}, s32[8,128]{1,0:T(8,128)S(1)}, u32[]{:S(2)}, u32[]{:S(2)}) %collective-permute-start.2) | collective-permute-done | bytes 4128 | tf_op jit(solution)/shard_map/ppermute | solution.py:23
  112.6 0.0 collective-permute-done.4.stats
  112.6 0.0 collective-permute-done.3.rows
  112.7 1.3 %copy-done.13 = bf16[2,128,4096]{2,1,0:T(8,128)(2,1)} copy-done((bf16[2,128,4096]{2,1,0:T(8,128)(2,1)}, bf16[2,128,4096]{2,1,0:T(8,128)(2,1)S(1)}, u32[]{:S(2)}) %copy-start.13) | copy-done | bytes 2097176
  114.0 0.0 copy-done.5
  114.0 0.0 copy-done.6
  114.0 9.6 %arrived_rows.1 = (bf16[1,768,512]{2,1,0:T(8,128)(2,1)}, bf16[1,768,512]{2,1,0:T(8,128)(2,1)}) custom-call(s32[8,128]{1,0:T(8,128)S(1)} %collective-permute-done.2.count, bf16[2,128,4096]{2,1,0:T(8,128)(2,1)} %copy-done.13, f32[16,1024]{1,0:T(8,128)S(1)} %collective-permute-done.4.stats, bf16[768,512]{1,0:T(8,128)(2,1)S(1)} %bitcast.5, ...), custom_call_target="tpu_custom_call" | custom-call | tf_op jit(solution)/shard_map/arrived_rows/pallas_call | solution.py:299
  (10 shorter events, 0.0 us)
Async XLA Ops:
  0.6 1.2 copy-start
  1.9 1.2 copy-start.1
  3.1 0.7 copy-start.9
  3.7 0.7 copy-start.10
  4.4 0.7 copy-start.11
  5.1 0.7 copy-start.12
  5.7 3.6 %copy-start.2 = (bf16[1,768,512]{2,1,0:T(8,128)(2,1)S(1)}, bf16[1,768,512]{2,1,0:T(8,128)(2,1)}, u32[]{:S(2)}) copy-start(bf16[1,768,512]{2,1,0:T(8,128)(2,1)} %param.13) | copy-start | bytes 2359300
  5.7 4.2 %copy-start.3 = (bf16[1,768,512]{2,1,0:T(8,128)(2,1)S(1)}, bf16[1,768,512]{2,1,0:T(8,128)(2,1)}, u32[]{:S(2)}) copy-start(bf16[1,768,512]{2,1,0:T(8,128)(2,1)} %param.14) | copy-start | bytes 2359300
  5.7 6.6 %copy-start.7 = (bf16[128,512]{1,0:T(8,128)(2,1)S(1)}, bf16[128,512]{1,0:T(8,128)(2,1)}, u32[]{:S(2)}) copy-start(bf16[128,512]{1,0:T(8,128)(2,1)} %refs_8_.1) | copy-start | bytes 393220
  5.7 6.6 %copy-start.8 = (bf16[128,512]{1,0:T(8,128)(2,1)S(1)}, bf16[128,512]{1,0:T(8,128)(2,1)}, u32[]{:S(2)}) copy-start(bf16[128,512]{1,0:T(8,128)(2,1)} %refs_9_.3) | copy-start | bytes 393220
  7.8 80.4 %copy-start.4 = (bf16[2,128,4096]{2,1,0:T(8,128)(2,1)}, bf16[2,128,4096]{2,1,0:T(8,128)(2,1)S(1)}, u32[]{:S(2)}) copy-start(bf16[2,128,4096]{2,1,0:T(8,128)(2,1)S(1)} %get-tuple-element.21.refs_5_) | copy-start | bytes 6291460
  7.8 104.8 %collective-permute-start.3 = (bf16[2,128,4096]{2,1,0:T(8,128)(2,1)S(1)}, bf16[2,128,4096]{2,1,0:T(8,128)(2,1)S(1)}, u32[]{:S(2)}, u32[]{:S(2)}) collective-permute-start(bf16[2,128,4096]{2,1,0:T(8,128)(2,1)S(1)} %get-tuple-element.21.refs_5_), channel_id=1, source_target_pairs={{0,14},{2,0},{4,2},{6,4},{8,6},{10,8},{12,10},{14,12},{1,15},{3,1}... | collective-permute-start | bytes 6291464 | tf_op jit(solution)/shard_map/ppermute | solution.py:23
  9.3 62.9 %collective-permute-start = (bf16[768,512]{1,0:T(8,128)(2,1)S(1)}, bf16[768,512]{1,0:T(8,128)(2,1)S(1)}, u32[]{:S(2)}, u32[]{:S(2)}) collective-permute-start(bf16[768,512]{1,0:T(8,128)(2,1)S(1)} %bitcast.3), channel_id=1, source_target_pairs={{0,2},{2,4},{4,6},{6,8},{8,10},{10,12},{12,14},{14,0},{1,3},{3,5},... | collective-permute-start | bytes 2359304 | tf_op jit(solution)/shard_map/ppermute | solution.py:23
  9.9 78.3 %collective-permute-start.1 = (bf16[768,512]{1,0:T(8,128)(2,1)S(1)}, bf16[768,512]{1,0:T(8,128)(2,1)S(1)}, u32[]{:S(2)}, u32[]{:S(2)}) collective-permute-start(bf16[768,512]{1,0:T(8,128)(2,1)S(1)} %bitcast.6), channel_id=1, source_target_pairs={{0,2},{2,4},{4,6},{6,8},{8,10},{10,12},{12,14},{14,0},{1,3},{3,5},... | collective-permute-start | bytes 2359304 | tf_op jit(solution)/shard_map/ppermute | solution.py:23
  88.2 25.8 %copy-start.5 = (f32[768,512]{1,0:T(8,128)S(1)}, f32[768,512]{1,0:T(8,128)}, u32[]{:S(2)}) copy-start(f32[768,512]{1,0:T(8,128)} %get-tuple-element.32.own_key) | copy-start | bytes 4718596
  88.2 25.8 %copy-start.6 = (f32[768,512]{1,0:T(8,128)S(1)}, f32[768,512]{1,0:T(8,128)}, u32[]{:S(2)}) copy-start(f32[768,512]{1,0:T(8,128)} %get-tuple-element.33.own_value) | copy-start | bytes 4718596
  102.8 9.9 %collective-permute-start.4 = (f32[16,1024]{1,0:T(8,128)S(1)}, f32[16,1024]{1,0:T(8,128)S(1)}, u32[]{:S(2)}, u32[]{:S(2)}) collective-permute-start(f32[16,1024]{1,0:T(8,128)S(1)} %get-tuple-element.31), channel_id=1, source_target_pairs={{0,14},{2,0},{4,2},{6,4},{8,6},{10,8},{12,10},{14,12},{1,15},{3,1}... | collective-permute-start | bytes 196616 | tf_op jit(solution)/shard_map/ppermute | solution.py:23
  105.2 7.5 %collective-permute-start.2 = (s32[8,128]{1,0:T(8,128)S(1)}, s32[8,128]{1,0:T(8,128)S(1)}, u32[]{:S(2)}, u32[]{:S(2)}) collective-permute-start(s32[8,128]{1,0:T(8,128)S(1)} %get-tuple-element.30), channel_id=1, source_target_pairs={{0,14},{2,0},{4,2},{6,4},{8,6},{10,8},{12,10},{14,12},{1,15},{3,1}... | collective-permute-start | bytes 12296 | tf_op jit(solution)/shard_map/ppermute | solution.py:23
  112.7 1.3 %copy-start.13 = (bf16[2,128,4096]{2,1,0:T(8,128)(2,1)}, bf16[2,128,4096]{2,1,0:T(8,128)(2,1)S(1)}, u32[]{:S(2)}) copy-start(bf16[2,128,4096]{2,1,0:T(8,128)(2,1)S(1)} %collective-permute-done.3.rows) | copy-start | bytes 6291460
